TPU v7x, 256 devices: a whole 4x4x8 slice. The times are simulated.
256 devices in a mesh: traj: 8 (over y, core), feat: 32 (over x, z).
Axes of the slice: x: 4, y: 4, z: 8, core: 2. Of those that a mesh axis runs over, the one named last changes fastest.
Arguments:
- frame_values: bfloat16 [40960, 8, 128], P(('traj', 'feat')), may hold values from 0 to 2
- frame_blocks: int32 [40960, 8], P(('traj', 'feat')), may hold values from 0 to 31, all different within a row
- lag_pairs: int32 [32768, 2], P(('traj', 'feat')), may hold values from 0 to 159, as said below
Outputs:
- cov_inst: float32 [4096, 4096], P('traj', 'feat')
- cov_lag: float32 [4096, 4096], P('traj', 'feat')
Inputs may be any that keep to these rules, and one draw needn't show every extreme that they name: `frame_blocks`: the 8 blocks of one frame are different. `lag_pairs`: on each device the first entries take every value of 0 to 127 once; the second entry lies 1 to 32 frames after the first.
All inputs are finite; a program needn't handle non-finite values.
Results may differ from a plain program's by a relative error of at most 0.0003.
Values may be sent and summed in bfloat16 or wider, within the bound.
A program may use at most 256 MiB of HBM per device.

v0:
```python
import jax
import jax.numpy as jnp
from jax import lax
from jax.sharding import PartitionSpec as P

NF = 4096
BLOCK = 128


def spread(values, blocks, count_blocks):
    onehot = (
        blocks[:, :, None] == jnp.arange(count_blocks, dtype=jnp.int32)[None, None, :]
    ).astype(jnp.bfloat16)
    filled = jnp.einsum("rkn,rkb->rnb", onehot, values, preferred_element_type=jnp.float32)
    return filled.astype(jnp.bfloat16).reshape(values.shape[0], count_blocks * values.shape[2])


def pair_ends(values, blocks, pair_rows, frames_per, pairs_per, count_blocks):
    offsets = jnp.arange(pair_rows.shape[0], dtype=jnp.int32) // pairs_per * frames_per
    first_index = pair_rows[:, 0] + offsets
    second_index = pair_rows[:, 1] + offsets
    start_rows = spread(values[first_index], blocks[first_index], count_blocks)
    lagged_rows = spread(values[second_index], blocks[second_index], count_blocks)
    return (start_rows, lagged_rows)


def contract(left_side, right_side):
    return lax.dot_general(
        left_side, right_side, (((0,), (0,)), ((), ())), preferred_element_type=jnp.float32
    )


def column_sums(filled):
    unit_weights = jnp.ones((filled.shape[0],), jnp.bfloat16)
    return jnp.dot(unit_weights, filled, preferred_element_type=jnp.float32)


def on_device(frame_values, frame_blocks, lag_pairs):
    frames_per = frame_values.shape[0]
    pairs_per = lag_pairs.shape[0]
    count_blocks = NF // BLOCK
    traj_count = lax.axis_size("traj")
    feat_count = lax.axis_size("feat")
    pair_total = pairs_per * traj_count * feat_count
    row_width = NF // traj_count
    col_width = NF // feat_count
    row_first = lax.axis_index("traj") * row_width
    col_first = lax.axis_index("feat") * col_width
    gathered = (
        lax.all_gather(frame_values, "traj", axis=0, tiled=True),
        lax.all_gather(frame_blocks, "traj", axis=0, tiled=True),
        lax.all_gather(lag_pairs, "traj", axis=0, tiled=True),
    )
    start_rows, lagged_rows = pair_ends(
        gathered[0], gathered[1], gathered[2], frames_per, pairs_per, count_blocks
    )
    start_slab = lax.dynamic_slice_in_dim(start_rows, row_first, row_width, 1)
    start_cols = lax.slice_in_dim(start_rows, 0, col_width * lax.axis_size("feat"), axis=1)
    lagged_cols = lax.slice_in_dim(lagged_rows, 0, col_width * lax.axis_size("feat"), axis=1)
    moments = lax.psum_scatter(
        jnp.concatenate(
            [contract(start_cols, start_slab), contract(lagged_cols, start_slab)], axis=1
        ),
        "feat",
        scatter_dimension=0,
        tiled=True,
    )
    plain_sums = moments[:, :row_width].T
    lagged_sums = moments[:, row_width:].T
    own_start, own_lagged = pair_ends(
        frame_values, frame_blocks, lag_pairs, frames_per, pairs_per, count_blocks
    )
    start_sum, lagged_sum = lax.psum(
        (column_sums(own_start), column_sums(own_lagged)), ("traj", "feat")
    )
    mean_start = start_sum / pair_total
    mean_lagged = lagged_sum / pair_total
    mean_rows = lax.dynamic_slice_in_dim(mean_start, row_first, row_width, 0)
    mean_cols = lax.dynamic_slice_in_dim(mean_start, col_first, col_width, 0)
    lagged_cols = lax.dynamic_slice_in_dim(mean_lagged, col_first, col_width, 0)
    cov_inst = plain_sums / pair_total - mean_rows[:, None] * mean_cols[None, :]
    cov_lag = lagged_sums / pair_total - mean_rows[:, None] * lagged_cols[None, :]
    return (cov_inst, cov_lag)


def solution(mesh):
    in_specs = (
        P(("traj", "feat"), None, None),
        P(("traj", "feat"), None),
        P(("traj", "feat"), None),
    )
    out_specs = (P("traj", "feat"), P("traj", "feat"))
    return jax.shard_map(
        on_device, mesh=mesh, in_specs=in_specs, out_specs=out_specs, check_vma=False
    )
```

profile of v0, /device:TPU:1, one launch (start us, length us, event | category | flops | bytes accessed | tf_op | source)
XLA Modules:
  0.0 363.9 jit_solution(8188696037893392922)
XLA Ops:
  7.2 0.0 all-gather.3.cloned.1.call-start
  7.2 0.7 all-gather.3.cloned.1.call-update
  7.9 0.0 reduce-scatter.2.cloned.1.call-start
  8.0 16.0 %all-gather = s32[8,160,8]{1,2,0:T(8,128)S(1)} all-gather(s32[1,160,8]{1,2,0:T(8,128)} %bitcast.49), channel_id=1, replica_groups=mesh['traj'=8,'feat'=32] {'traj'}, dimensions={0}, use_global_device_ids=true | all-gather | bytes 46080 | tf_op jit(solution)/shard_map/all_gather | solution.py:51
  24.0 0.3 copy.8
  24.2 9.3 %all_gather.10 = s32[1024,2]{0,1:T(2,128)S(1)} all-gather(s32[128,2]{0,1:T(2,128)} %param.5), channel_id=1, replica_groups=mesh['traj'=8,'feat'=32] {'traj'}, dimensions={0}, use_global_device_ids=true | all-gather | bytes 9216 | tf_op jit(solution)/shard_map/all_gather | solution.py:52
  33.6 2.8 gather_fusion
  36.4 2.8 gather_fusion.2
  39.2 3.6 all-gather.3.cloned.1.call-done
  42.8 5.1 %gather_fusion.1 = bf16[1024,8,128]{2,1,0:T(8,128)(2,1)S(1)} fusion(bf16[1280,8,128]{2,1,0:T(8,128)(2,1)} %all-gather.3.cloned.1.call-done, s32[1024]{0:T(1024)S(1)} %broadcast_clamp_fusion.1), kind=kCustom, calls=%fused_computation.1 | custom fusion | bytes 4198400 | tf_op jit(solution)/shard_map/gather | solution.py:22
  47.9 7.8 %convolution_convert_fusion.1 = bf16[1024,32,128]{2,1,0:T(8,128)(2,1)} fusion(bf16[1024,8,128]{2,1,0:T(8,128)(2,1)S(1)} %gather_fusion.1, s32[1024,8]{1,0:T(8,128)S(1)} %gather_fusion), kind=kOutput, calls=%fused_computation.14 | convolution fusion | flops 71565312 | bytes 10518528 | tf_op jit(solution)/shard_map/rkn,rkb->rnb/dot_general | solution.py:14
  55.6 15.1 %copy.28 = bf16[128,8,32,128]{3,1,2,0:T(8,128)(2,1)} copy(bf16[128,8,32,128]{3,2,1,0:T(8,128)(2,1)} %bitcast.41) | data formatting | bytes 16777216
  70.7 5.1 %gather_fusion.3 = bf16[1024,8,128]{2,1,0:T(8,128)(2,1)S(1)} fusion(bf16[1280,8,128]{2,1,0:T(8,128)(2,1)} %all-gather.3.cloned.1.call-done, s32[1024]{0:T(1024)S(1)} %broadcast_clamp_fusion), kind=kCustom, calls=%fused_computation.3 | custom fusion | bytes 4198400 | tf_op jit(solution)/shard_map/gather | solution.py:23
  75.8 0.0 copy-start
  75.8 7.9 %convolution_convert_fusion = bf16[1024,32,128]{2,1,0:T(8,128)(2,1)S(1)} fusion(bf16[1024,8,128]{2,1,0:T(8,128)(2,1)S(1)} %gather_fusion.3, s32[1024,8]{1,0:T(8,128)S(1)} %gather_fusion.2), kind=kOutput, calls=%fused_computation.13 | convolution fusion | flops 71565312 | bytes 10518528 | tf_op jit(solution)/shard_map/rkn,rkb->rnb/dot_general | solution.py:14
  83.7 0.0 copy-done
  83.7 4.9 %fusion.12 = f32[4096,512]{0,1:T(8,128)S(1)} fusion(bf16[1024,4096]{1,0:T(8,128)(2,1)S(1)} %bitcast.42, s32[]{:T(128)S(6)} %select_n.60), kind=kOutput, calls=%fused_computation.28 | convolution fusion | flops 4294967296 | bytes 17825796 | tf_op jit(solution)/shard_map/dot_general | solution.py:28
  88.6 13.1 %fusion = f32[4096,512]{0,1:T(8,128)} fusion(bf16[128,8,32,128]{3,2,1,0:T(8,128)(2,1)S(1)} %bitcast.44, bf16[1024,4096]{1,0:T(8,128)(2,1)S(1)} %bitcast.43, s32[]{:T(128)S(6)} %select_n.60), kind=kOutput, calls=%fused_computation.9 | convolution fusion | flops 4294967296 | bytes 17825796 | tf_op jit(solution)/shard_map/dot_general | solution.py:28
  101.7 10.0 %pad_maximum_fusion = f32[4096,1024]{0,1:T(8,128)} fusion(f32[4096,512]{0,1:T(8,128)} %fusion, f32[4096,512]{0,1:T(8,128)S(1)} %fusion.12), kind=kLoop, calls=%fused_computation.8 | loop fusion | flops 4194304 | bytes 33554432 | tf_op jit(solution)/shard_map/concatenate | solution.py:61
  111.8 0.0 copy-start.2
  111.8 0.0 copy-start.3
  111.8 0.0 copy-start.1
  111.8 0.0 reduce-scatter.2.cloned.1.call-update
  111.8 0.7 copy-done.2
  112.5 0.1 copy.9
  112.6 0.0 copy-done.3
  112.6 0.2 copy-done.1
  112.8 0.7 gather_fusion.5
  113.5 0.6 gather_fusion.4
  114.1 0.6 gather_fusion.6
  114.8 0.7 gather_fusion.7
  115.5 0.9 convolution_convert_fusion.3
  116.4 0.4 fusion.8
  116.8 0.9 convolution_convert_fusion.2
  117.7 0.4 fusion.5
  118.1 78.1 %all-reduce = (f32[4096]{0:T(1024)S(1)}, f32[4096]{0:T(1024)S(1)}) all-reduce(f32[4096]{0:T(1024)S(1)} %bitcast.47, f32[4096]{0:T(1024)S(1)} %bitcast.48), channel_id=1, replica_groups=mesh['traj'=8,'feat'=32] {'traj','feat'}, use_global_device_ids=true, to_apply=%region_1.2 | all-reduce | flops 8192 | bytes 65536 | tf_op jit(solution)/shard_map/psum | solution.py:73
  196.2 0.1 dynamic_slice.13
  196.3 0.1 dynamic_slice.14
  196.4 0.1 dynamic-slice_multiply_fusion
  196.5 158.7 %reduce-scatter.2.cloned.1.call-done = f32[128,1024]{0,1:T(8,128)} async-done(((f32[4096,1024]{0,1:T(8,128)}), f32[128,1024]{0,1:T(8,128)}) %reduce-scatter.2.cloned.1.call-update) | async-done | bytes 524304 | tf_op jit(solution)/shard_map/reduce_scatter | solution.py:60
  355.1 2.0 fusion.15
  (6 shorter events, 0.0 us)
Async XLA Ops:
  7.2 35.6 %all-gather.3.cloned.1.call-start = ((), (), s32[]{:S(2)}) async-start(), calls=%async_computation.1 | async-start | bytes 2949120 | tf_op jit(solution)/shard_map/all_gather | solution.py:50
  7.9 347.2 %reduce-scatter.2.cloned.1.call-start = ((), (), s32[]{:S(2)}) async-start(), calls=%async_computation.2 | async-start | bytes 17301504 | tf_op jit(solution)/shard_map/reduce_scatter | solution.py:60
  75.8 7.9 %copy-start = (bf16[128,8,32,128]{3,1,2,0:T(8,128)(2,1)S(1)}, bf16[128,8,32,128]{3,1,2,0:T(8,128)(2,1)}, u32[]{:S(2)}) copy-start(bf16[128,8,32,128]{3,1,2,0:T(8,128)(2,1)} %copy.28) | copy-start | bytes 25165828
  111.8 0.7 copy-start.2
  111.8 0.8 copy-start.3
  111.8 1.0 copy-start.1
Sparse Core Ops, SparseCore 0:
  9.8 32.9 all-gather.2
  111.9 243.1 reduce-scatter.1
where the time goes:
time: 367 us; the launch traced here: 364 us
  waiting for transfers between devices  163 us (44%)
  blocking collectives  103 us (28%)
  matrix products  36.3 us (10%)
  local copies, waits for them, and re-layouts  34.9 us (10%)
  between operations  14.2 us (4%)
  other arithmetic  12.1 us (3%)
    reduce_scatter x1, waiting for transfers between devices, on_device(): lax.psum_scatter(jnp.concatenate([contract(start_cols, start_slab), contr...  159 us
    psum x1, blocking collectives, on_device(): lax.psum((column_sums(own_start), column_sums(own_lagged)), ('traj', 'fea...  78.1 us
    dot_general x2, matrix products, contract(): lax.dot_general(left_side, right_side, (((0,), (0,)), ((), ())), preferre...  18 us
    dot_general x4, matrix products, spread(): jnp.einsum('rkn,rkb->rnb', onehot, values, preferred_element_type=jnp.flo...  17.5 us
    unnamed x10, local copies, waits for them, and re-layouts  16 us
    all_gather x1, blocking collectives, on_device(): lax.all_gather(frame_blocks, 'traj', axis=0, tiled=True)  16 us
    concatenate x1, other arithmetic, on_device(): jnp.concatenate([contract(start_cols, start_slab), contract(lagged_cols,...  10 us
    all_gather x1, blocking collectives, on_device(): lax.all_gather(lag_pairs, 'traj', axis=0, tiled=True)  9.34 us
  transfers between devices with their start and end apart: 2, of which 2 were waited for; matrix products, arithmetic and copies ran while one was open for 3% of the time, Pallas kernels for 0%

commit v1 on v0

v1 whole, which is shorter than its diff:
```python
import functools

import jax
import jax.numpy as jnp
from jax import lax
from jax.experimental import pallas as pl
from jax.experimental.pallas import tpu as pltpu
from jax.sharding import PartitionSpec as P

MESH = pl.DeviceIdType.MESH
F32, BF16 = jnp.float32, jnp.bfloat16
NX, NY, NZ = 4, 4, 8
B = 128
SLOTS = 8
FRAMES = 160
EXTRA = FRAMES - B
IDS = 10 * B
PACKET = IDS + 16
HALF = 5 * B
CHUNK = 4 * B + 8
CUT = 264
PAIRS = 32768
NT = (((1,), (1,)), ((), ()))


def place():
    t, f = lax.axis_index("traj"), lax.axis_index("feat")
    return f // NZ, t // 2, f % NZ, t % 2


def prepare(values, blocks, pairs, packet, plain, index):
    plain[...] = values[...].astype(F32).reshape(FRAMES * SLOTS, B)
    for k in range(SLOTS):
        tile = plain[pl.ds(k, B, stride=SLOTS), :]
        packet[k * B : (k + 1) * B, :] = tile.T.astype(BF16)
    for g in range(2):
        tile = jnp.concatenate(
            [plain[pl.ds(B * SLOTS + 4 * g + i, EXTRA, stride=SLOTS), :] for i in range(4)], axis=0
        )
        packet[(SLOTS + g) * B : (SLOTS + g + 1) * B, :] = tile.T.astype(BF16)
    index[...] = jnp.zeros_like(index)
    index[:, 0:SLOTS] = blocks[...].astype(F32)
    first = index[0:B, :].T[0:SLOTS, :]
    rest = jnp.concatenate([index[B:FRAMES, :]] * 4, axis=0).T
    lane = lax.broadcasted_iota(jnp.int32, (1, B), 1) // EXTRA
    rows = [first]
    for g in range(2):
        row = jnp.zeros((1, B), F32)
        for i in range(4):
            row = jnp.where(lane == i, rest[4 * g + i : 4 * g + i + 1, :], row)
        rows.append(row)
    start, lagged = pairs[:, 0:1], pairs[:, 1:2]
    here = start == lax.broadcasted_iota(jnp.int32, (B, B), 1)
    rows.append(jnp.sum(jnp.where(here, lagged.astype(F32), 0.0), axis=0, keepdims=True))
    rows.append(jnp.zeros((5, B), F32))
    packet[IDS:PACKET, :] = jnp.concatenate(rows, axis=0).astype(BF16)


def fill(source, lanes, core, z, dense_rows, dense_cols, picked, picks):
    ids = source[IDS:PACKET, :].astype(F32)
    wide = [jnp.broadcast_to(ids[k : k + 1, :], (16, B)).astype(BF16) for k in range(SLOTS + 2)]
    none = jnp.zeros((16, B), BF16)

    def block(number, put):
        want = jnp.full((16, B), number, jnp.int32).astype(F32).astype(BF16)
        masks = [w == want for w in wide[:SLOTS]]
        for j in range(0, B, 16):
            got = none
            for k in range(SLOTS):
                got = jnp.where(masks[k], source[k * B + j : k * B + j + 16, :], got)
            put(j, got)
        return want

    def rows_of(n, carry):
        def put(j, got):
            dense_rows[pl.ds(pl.multiple_of(n * B + j, 16), 16), lanes] = got

        block(n // 4 * NZ + core * 4 + n % 4, put)
        return carry

    lax.fori_loop(0, 4 * NY, rows_of, 0)

    def cols_of(n, carry):
        def put(j, got):
            dense_cols[n, j : j + 16, lanes] = got
            picked[pl.ds(pl.multiple_of(n * B + j, 16), 16), 0:B] = got

        want = block(n * NZ + z, put)
        for g in range(2):
            mask = wide[SLOTS + g] == want
            for j in range(0, B, 16):
                tile = source[(SLOTS + g) * B + j : (SLOTS + g) * B + j + 16, :]
                picked[pl.ds(pl.multiple_of(n * B + j, 16), 16), (g + 1) * B : (g + 2) * B] = (
                    jnp.where(mask, tile, none)
                )
        return carry

    lax.fori_loop(0, NX, cols_of, 0)
    down = lax.broadcasted_iota(jnp.int32, (B, B), 0).astype(F32)
    rest = (lax.broadcasted_iota(jnp.int32, (B, B), 0) % EXTRA + B).astype(F32)
    lag = jnp.broadcast_to(ids[SLOTS + 2 : SLOTS + 3, :], (B, B))
    picks[0:B, :] = jnp.where(lag == down, 1.0, 0.0).astype(BF16)
    tail = jnp.where(lag == rest, 1.0, 0.0).astype(BF16)
    picks[B : 2 * B, :] = tail
    picks[2 * B : 3 * B, :] = tail

    def lags_of(n, carry):
        part = picked[pl.ds(pl.multiple_of(n * B, B), B), :]
        dense_cols[n, B : 2 * B, lanes] = jnp.dot(
            part, picks[...], preferred_element_type=F32
        ).astype(BF16)
        return carry

    lax.fori_loop(0, NX, lags_of, 0)


def multiply(first, depth, dense_rows, dense_cols, inst, lag, row_sums, col_sums):
    def tile(n, carry):
        x, y = n // NY, n % NY
        rows = pl.ds(pl.multiple_of(y * 4 * B, 4 * B), 4 * B)
        out = lax.dot_general(
            dense_rows[rows, 0:depth], dense_cols[x, :, 0:depth], NT, preferred_element_type=F32
        )
        if first:
            inst[x, y, 0 : 4 * B, :] = out[:, 0:B]
            lag[y, x, 0 : 4 * B, :] = out[:, B : 2 * B]
        else:
            inst[x, y, 0 : 4 * B, :] += out[:, 0:B]
            lag[y, x, 0 : 4 * B, :] += out[:, B : 2 * B]
        return carry

    lax.fori_loop(0, NX * NY, tile, 0)

    def row_tile(y, carry):
        rows = pl.ds(pl.multiple_of(y * 4 * B, 4 * B), 4 * B)
        out = lax.dot_general(
            dense_rows[rows, 0:depth], jnp.ones((B, depth), BF16), NT, preferred_element_type=F32
        )
        if first:
            row_sums[rows, :] = out
        else:
            row_sums[rows, :] += out
        return carry

    lax.fori_loop(0, NY, row_tile, 0)

    def col_tile(x, carry):
        out = lax.dot_general(
            jnp.ones((8, depth), BF16), dense_cols[x, :, 0:depth], NT, preferred_element_type=F32
        )
        if first:
            col_sums[x] = out
        else:
            col_sums[x] += out
        return carry

    lax.fori_loop(0, NX, col_tile, 0)


def sums_into(row_sums, col_sums, inst, lag):
    diagonal = lax.broadcasted_iota(jnp.int32, (B, B), 0) == lax.broadcasted_iota(
        jnp.int32, (B, B), 1
    )

    def of_rows(y, carry):
        flat = []
        for i in range(4):
            tile = row_sums[pl.ds(pl.multiple_of(y * 4 * B + i * B, B), B), :]
            flat.append(jnp.sum(jnp.where(diagonal, tile, 0.0), axis=0, keepdims=True))

        def of_cols(x, inner):
            sums = col_sums[x]
            inst[x, y, 4 * B : CHUNK, :] = jnp.concatenate(flat + [sums[0:4, 0:B]], axis=0)
            lag[y, x, 4 * B : CHUNK, :] = jnp.concatenate(flat + [sums[0:4, B : 2 * B]], axis=0)
            return inner

        return lax.fori_loop(0, NX, of_cols, carry)

    lax.fori_loop(0, NY, of_rows, 0)


def add_rows(target, addends, start, count):
    step = 8 if count % 64 else 64

    def body(n, carry):
        rows = pl.ds(pl.multiple_of(start + n * step, 8), step)
        total = target[rows, :]
        for a in addends:
            total = total + a[rows, :]
        target[rows, :] = total
        return carry

    lax.fori_loop(0, count // step, body, 0)


def kernel(
    values, blocks, pairs, inst_out, lag_out,
    plain, index, ring, pair, dense_rows, dense_cols, picked, picks,
    inst, lag, row_sums, col_sums, far1, near1, far2, near2,
    ring_send, ring_recv, pair_send, pair_recv, rs_send, rs_recv,
):
    x, y, z, core = place()

    def device(dx=0, dy=0, dz=0, dc=0):
        return (
            lax.rem(y + dy + NY, NY) * 2 + lax.rem(core + dc, 2),
            lax.rem(x + dx + NX, NX) * NZ + lax.rem(z + dz + NZ, NZ),
        )

    def send(source, target, send_sem, recv_sem, to):
        copy = pltpu.make_async_remote_copy(
            src_ref=source, dst_ref=target, send_sem=send_sem, recv_sem=recv_sem,
            device_id=to, device_id_type=MESH,
        )
        copy.start()
        return copy

    up, down, other = device(dz=1), device(dz=-1), device(dc=1)
    barrier = pltpu.get_barrier_semaphore()
    for to in (up, down, other, device(dx=1), device(dx=-1), device(dy=1), device(dy=-1)):
        pl.semaphore_signal(barrier, inc=1, device_id=to, device_id_type=MESH)

    prepare(values, blocks, pairs, ring.at[0], plain, index)
    pl.semaphore_wait(barrier, 7)

    started = []

    def share(slot, rows, sem):
        started.append(
            send(ring.at[slot, rows], pair.at[slot, rows], pair_send.at[sem], pair_recv.at[sem], other)
        )
        return started[-1]

    whole = pl.ds(0, PACKET)
    low, high = pl.ds(0, HALF), pl.ds(HALF, PACKET - HALF)
    right = send(ring.at[0], ring.at[1], ring_send.at[1], ring_recv.at[1], up)
    left = send(ring.at[0], ring.at[4], ring_send.at[4], ring_recv.at[4], down)
    shared = share(0, whole, 0)

    def fill_from(buffer, slot, position):
        lanes = pl.ds(position * B, B)
        fill(buffer.at[slot], lanes, core, z, dense_rows, dense_cols, picked, picks)

    def product(first, depth):
        multiply(first, depth, dense_rows, dense_cols, inst, lag, row_sums, col_sums)

    fill_from(ring, 0, 0)
    shared.wait_recv()
    fill_from(pair, 0, 1)
    product(True, 2 * B)

    for s in range(1, 4):
        right.wait_recv()
        started.append(right)
        if s < 3:
            right = send(ring.at[s], ring.at[s + 1], ring_send.at[s + 1], ring_recv.at[s + 1], up)
        else:
            right = send(ring.at[s, low], ring.at[7, low], ring_send.at[7], ring_recv.at[7], up)
        left.wait_recv()
        started.append(left)
        if s < 3:
            left = send(ring.at[3 + s], ring.at[4 + s], ring_send.at[4 + s], ring_recv.at[4 + s], down)
        else:
            left = send(ring.at[6, high], ring.at[7, high], ring_send.at[8], ring_recv.at[8], down)
        shared = [share(s, whole, s), share(3 + s, whole, 3 + s)]

        def from_ring(n, carry, s=s):
            fill_from(ring, s + 3 * n, n)
            return carry

        lax.fori_loop(0, 2, from_ring, 0)
        for copy in shared:
            copy.wait_recv()

        def from_pair(n, carry, s=s):
            fill_from(pair, s + 3 * n, 2 + n)
            return carry

        lax.fori_loop(0, 2, from_pair, 0)
        product(False, 4 * B)

    right.wait_recv()
    shared = [share(7, low, 7)]
    left.wait_recv()
    shared.append(share(7, high, 8))
    started += [right, left]
    fill_from(ring, 7, 0)
    for copy in shared:
        copy.wait_recv()
    fill_from(pair, 7, 1)
    product(False, 2 * B)
    sums_into(row_sums, col_sums, inst, lag)

    def axes(which):
        if which == 0:
            return inst, x, y, (device(dx=1), device(dx=-1)), (device(dy=1), device(dy=-1))
        return lag, y, x, (device(dy=1), device(dy=-1)), (device(dx=1), device(dx=-1))

    halves = (pl.ds(0, 2), pl.ds(2, 2))
    cuts = (pl.ds(0, CUT), pl.ds(CUT, CHUNK - CUT))

    def rs_copy(which, number, source, target, to):
        started.append(
            send(source, target, rs_send.at[which, number], rs_recv.at[which, number], to)
        )
        return started[-1]

    far, near, joint = {}, {}, {}
    for which in range(2):
        acc, a, _, to, _ = axes(which)
        for d in range(2):
            far[which, d] = rs_copy(
                which, d, acc.at[lax.rem(a + 2, 4), halves[d]], far1.at[which, d], to[d]
            )
    for which in range(2):
        acc, a, _, to, _ = axes(which)
        for d in range(2):
            near[which, d] = rs_copy(
                which, 2 + d, acc.at[lax.rem(a + 1 + 2 * d, 4), halves[1 - d]],
                near1.at[which, d, halves[1 - d]], to[d],
            )
    for d in range(2):
        for which in range(2):
            acc, a, _, to, _ = axes(which)
            far[which, d].wait_recv()
            target = lax.rem(a + 1 + 2 * d, 4)
            for h in range(2):
                add_rows(acc.at[target, 2 * d + h], [far1.at[which, d, h]], 0, CHUNK)
            joint[which, d] = rs_copy(
                which, 4 + d, acc.at[target, halves[d]], near1.at[which, d, halves[d]], to[d]
            )
    for which in range(2):
        acc, a, _, _, _ = axes(which)
        for d in range(2):
            near[which, d].wait_recv()
            joint[which, d].wait_recv()

        def summed(h, carry, which=which, acc=acc, a=a):
            add_rows(acc.at[a, h], [near1.at[which, 0, h], near1.at[which, 1, h]], 0, CHUNK)
            return carry

        lax.fori_loop(0, 4, summed, 0)
        acc, a, b, _, to = axes(which)
        for d in range(2):
            far[which, d] = rs_copy(
                which, 6 + d, acc.at[a, lax.rem(b + 2, 4), cuts[d]], far2.at[which, d, cuts[d]], to[d]
            )
        for d in range(2):
            near[which, d] = rs_copy(
                which, 8 + d, acc.at[a, lax.rem(b + 1 + 2 * d, 4), cuts[1 - d]],
                near2.at[which, d, cuts[1 - d]], to[d],
            )
    for which in range(2):
        acc, a, b, _, to = axes(which)
        for d in range(2):
            far[which, d].wait_recv()
            target = lax.rem(b + 1 + 2 * d, 4)
            add_rows(
                acc.at[a, target], [far2.at[which, d]], CUT * d, CUT if d == 0 else CHUNK - CUT
            )
            joint[which, d] = rs_copy(
                which, 10 + d, acc.at[a, target, cuts[d]], near2.at[which, d, cuts[d]], to[d]
            )
    for which, out in ((0, inst_out), (1, lag_out)):
        acc, a, b, _, _ = axes(which)
        for d in range(2):
            near[which, d].wait_recv()
            joint[which, d].wait_recv()
        out[...] = acc[a, b] + near2[which, 0] + near2[which, 1]
    for copy in started:
        copy.wait_send()


def on_device(frame_values, frame_blocks, lag_pairs):
    chunk = jax.ShapeDtypeStruct((CHUNK, B), F32)
    vmem = pl.BlockSpec(memory_space=pltpu.VMEM)
    inst, lag = pl.pallas_call(
        kernel,
        out_shape=(chunk, chunk),
        in_specs=[vmem] * 3,
        out_specs=(vmem, vmem),
        scratch_shapes=[
            pltpu.VMEM((FRAMES * SLOTS, B), F32),
            pltpu.VMEM((FRAMES, B), F32),
            pltpu.VMEM((NZ, PACKET, B), BF16),
            pltpu.VMEM((NZ, PACKET, B), BF16),
            pltpu.VMEM((4 * NY * B, 4 * B), BF16),
            pltpu.VMEM((NX, 2 * B, 4 * B), BF16),
            pltpu.VMEM((NX * B, 3 * B), BF16),
            pltpu.VMEM((3 * B, B), BF16),
            pltpu.VMEM((NX, NY, CHUNK, B), F32),
            pltpu.VMEM((NY, NX, CHUNK, B), F32),
            pltpu.VMEM((4 * NY * B, B), F32),
            pltpu.VMEM((NX, 8, 2 * B), F32),
            pltpu.VMEM((2, 2, 2, CHUNK, B), F32),
            pltpu.VMEM((2, 2, 4, CHUNK, B), F32),
            pltpu.VMEM((2, 2, CHUNK, B), F32),
            pltpu.VMEM((2, 2, CHUNK, B), F32),
            pltpu.SemaphoreType.DMA((9,)),
            pltpu.SemaphoreType.DMA((9,)),
            pltpu.SemaphoreType.DMA((9,)),
            pltpu.SemaphoreType.DMA((9,)),
            pltpu.SemaphoreType.DMA((2, 12)),
            pltpu.SemaphoreType.DMA((2, 12)),
        ],
        compiler_params=pltpu.CompilerParams(
            collective_id=0, has_side_effects=True, vmem_limit_bytes=56 << 20
        ),
        name="covariances",
    )(frame_values, frame_blocks, lag_pairs)
    rows = inst[4 * B : 4 * B + 4].reshape(4 * B, 1) / PAIRS
    cov_inst = inst[: 4 * B] / PAIRS - rows * (inst[4 * B + 4 : 4 * B + 5] / PAIRS)
    cov_lag = lag[: 4 * B] / PAIRS - rows * (lag[4 * B + 4 : 4 * B + 5] / PAIRS)
    return cov_inst, cov_lag


def solution(mesh):
    spec = P(("traj", "feat"))
    return jax.shard_map(
        on_device,
        mesh=mesh,
        in_specs=(spec, spec, spec),
        out_specs=(P("traj", "feat"), P("traj", "feat")),
        check_vma=False,
    )
```

time: 367 us -> 124 us (0.34)
  waiting for transfers between devices: 163 us -> 0 us
  Pallas kernels: 0 us -> 118 us
  blocking collectives: 103 us -> 0 us
  matrix products: 36.3 us -> 0 us
  local copies, waits for them, and re-layouts: 34.9 us -> 2.17 us
  between operations: 14.2 us -> 0.65 us
  other arithmetic: 12.1 us -> 3.32 us
    reduce_scatter x1 -> x0, waiting for transfers between devices: 159 us -> none  [on_device(): lax.psum_scatter(jnp.concatenate([contract(start_cols, start_slab), contr...]
    pallas_call x0 -> x1, Pallas kernels: none -> 118 us  [on_device(): pl.pallas_call(kernel, out_shape=(chunk, chunk), in_specs=[vmem] * 3, out...]
    psum x1 -> x0, blocking collectives: 78.1 us -> none  [on_device(): lax.psum((column_sums(own_start), column_sums(own_lagged)), ('traj', 'fea...]
    dot_general x8 -> x0, matrix products: 36.3 us -> none  [the longest x2 18 us: contract(): lax.dot_general(left_side, right_side, (((0,), (0,)), ((), ())), preferre...]
    all_gather x2 -> x0, blocking collectives: 25.4 us -> none  [the longest x1 16 us: on_device(): lax.all_gather(frame_blocks, 'traj', axis=0, tiled=True)]
    gather x8 -> x0, local copies, waits for them, and re-layouts: 18.4 us -> none  [the longest x4 9.22 us: pair_ends(): start_rows = spread(values[first_index], blocks[first_index], count_blocks)]
    unnamed x10 -> x4, local copies, waits for them, and re-layouts: 16 us -> 2.17 us
    concatenate x1 -> x0, other arithmetic: 10 us -> none  [on_device(): jnp.concatenate([contract(start_cols, start_slab), contract(lagged_cols,...]
  transfers between devices with their start and end apart: 2 -> 0, of which waited for: 2 -> 0; matrix products, arithmetic and copies ran while one was open for 3% -> 0% of each run, Pallas kernels for 0% -> 0%
where the time goes in v1:
time: 124 us
  Pallas kernels  118 us (95%)
  other arithmetic  3.32 us (3%)
  local copies, waits for them, and re-layouts  2.17 us (2%)
    pallas_call x1, Pallas kernels, on_device(): pl.pallas_call(kernel, out_shape=(chunk, chunk), in_specs=[vmem] * 3, out...  118 us

profile of v1, /device:TPU:1, one launch (start us, length us, event | category | flops | bytes accessed | tf_op | source)
XLA Modules:
  0.0 124.2 jit_solution(14647350867850332036)
XLA Ops:
  0.6 0.0 copy-start
  0.6 1.4 %copy.6.pairs = s32[128,2]{1,0:T(8,128)} copy(s32[128,2]{0,1:T(2,128)} %param.5) | data formatting | bytes 2048 | tf_op args[2]
  2.1 0.0 copy-done
  2.1 0.7 copy.5.blocks
  2.8 118.1 %covariances.1 = (f32[520,128]{1,0:T(8,128)}, f32[520,128]{1,0:T(8,128)}) custom-call(bf16[160,8,128]{2,1,0:T(8,128)(2,1)} %values.1, s32[160,8]{1,0:T(8,128)} %copy.5.blocks, s32[128,2]{1,0:T(8,128)} %copy.6.pairs), custom_call_target="tpu_custom_call" | custom-call | tf_op jit(solution)/shard_map/covariances/pallas_call | solution.py:377
  120.9 0.7 multiply_bitcast_fusion.1
  121.6 0.7 multiply_bitcast_fusion
  122.3 2.0 %multiply_subtract_fusion = (f32[512,128]{1,0:T(8,128)}, f32[512,128]{1,0:T(8,128)}) fusion(f32[520,128]{1,0:T(8,128)} %get-tuple-element.5, f32[128]{0:T(128)S(1)} %get-tuple-element.8, f32[512]{0:T(512)S(1)} %multiply_bitcast_fusion, f32[128]{0:T(128)S(1)} %get-tuple-element.9, f32[520,128]{1,0:T(8,128)} %get-tuple-element.4), kind=kLoop, calls=%fused_computation | loop fusion | flops 393216 | bytes 1051648 | tf_op jit(solution)/shard_map/sub | solution.py:413
Async XLA Ops:
  0.6 1.4 %copy-start = (s32[160,8]{0,1:T(8,128)S(1)}, s32[160,8]{0,1:T(8,128)}, u32[]{:S(2)}) copy-start(s32[160,8]{0,1:T(8,128)} %param.4) | copy-start | bytes 15364

commit v2 on v1

v2 whole, which is shorter than its diff:
```python
import jax
import jax.numpy as jnp
from jax import lax
from jax.experimental import pallas as pl
from jax.experimental.pallas import tpu as pltpu
from jax.sharding import PartitionSpec as P

MESH = pl.DeviceIdType.MESH
F32, BF16, I16, I32 = jnp.float32, jnp.bfloat16, jnp.int16, jnp.int32
NX, NY, NZ = 4, 4, 8
B = 128
SLOTS = 8
FRAMES = 160
EXTRA = FRAMES - B
IDS = 10 * B
PACKET = IDS + 16
HALF = 5 * B
ROWS = 4 * NY * B
COLS = 2 * NX * B
GROUP = 2 * NZ * B
PAIRS = NX * NY * GROUP
FAR = 8 * B + 16
NEAR = 2 * B + 16
STEPS = 16.0
TOP = 32512.0
NT = (((1,), (1,)), ((), ()))
TN = (((0,), (0,)), ((), ()))


def place():
    t, f = lax.axis_index("traj"), lax.axis_index("feat")
    return f // NZ, t // 2, f % NZ, t % 2


def prepare(values, blocks, pairs, packet, plain, index):
    plain[...] = values[...].astype(F32).reshape(FRAMES * SLOTS, B)
    for k in range(SLOTS):
        tile = plain[pl.ds(k, B, stride=SLOTS), :]
        packet[k * B : (k + 1) * B, :] = tile.T.astype(BF16)
    for g in range(2):
        tile = jnp.concatenate(
            [plain[pl.ds(B * SLOTS + 4 * g + i, EXTRA, stride=SLOTS), :] for i in range(4)], axis=0
        )
        packet[(SLOTS + g) * B : (SLOTS + g + 1) * B, :] = tile.T.astype(BF16)
    rows = [blocks[:, 0:B].astype(F32)]
    index[...] = jnp.zeros_like(index)
    index[:, 0:EXTRA] = blocks[:, B:FRAMES].astype(F32)
    rest = index[...]
    lane = lax.broadcasted_iota(I32, (1, B), 1) // EXTRA
    wide = rest
    for i in range(1, 4):
        wide = wide + pltpu.roll(rest, i * EXTRA, 1)
    for g in range(2):
        row = jnp.zeros((1, B), F32)
        for i in range(4):
            row = jnp.where(lane == i, wide[4 * g + i : 4 * g + i + 1, :], row)
        rows.append(row)
    start = jnp.broadcast_to(pairs[0:1, :], (B, B))
    here = jnp.where(start == lax.broadcasted_iota(I32, (B, B), 0), 1.0, 0.0).astype(BF16)
    lagged = jnp.broadcast_to(pairs[1:2, :], (16, B)).astype(F32).astype(BF16)
    rows.append(lax.dot_general(lagged, here, NT, preferred_element_type=F32)[0:1, :])
    rows.append(jnp.zeros((5, B), F32))
    packet[IDS:PACKET, :] = jnp.concatenate(rows, axis=0).astype(BF16)


def fill(source, lanes, core, z, dense_rows, dense_cols, picked, picks):
    ids = source[IDS:PACKET, :].astype(F32)
    wide = [jnp.broadcast_to(ids[k : k + 1, :], (16, B)).astype(BF16) for k in range(SLOTS + 2)]
    none = jnp.zeros((16, B), BF16)

    def block(number, put):
        want = jnp.full((16, B), number, I32).astype(F32).astype(BF16)
        masks = [w == want for w in wide[:SLOTS]]
        for j in range(0, B, 16):
            got = none
            for k in range(SLOTS):
                got = jnp.where(masks[k], source[k * B + j : k * B + j + 16, :], got)
            put(j, got)
        return want

    lag = jnp.broadcast_to(ids[SLOTS + 2 : SLOTS + 3, :], (B, B))
    down = lax.broadcasted_iota(I32, (B, B), 0)
    picks[0:B, :] = jnp.where(lag == down.astype(F32), 1.0, 0.0).astype(BF16)
    picks[B : 2 * B, :] = jnp.where(lag == (down % EXTRA + B).astype(F32), 1.0, 0.0).astype(BF16)

    def cols_of(n, carry):
        def put(j, got):
            dense_cols[pl.ds(pl.multiple_of(n * 2 * B + j, 16), 16), lanes] = got
            picked[pl.ds(pl.multiple_of(n * B + j, 16), 16), 0:B] = got

        want = block(n * NZ + z, put)
        masks = [wide[SLOTS + g] == want for g in range(2)]
        for j in range(0, B, 16):
            got = none
            for g in range(2):
                tile = source[(SLOTS + g) * B + j : (SLOTS + g) * B + j + 16, :]
                got = jnp.where(masks[g], tile, got)
            picked[pl.ds(pl.multiple_of(n * B + j, 16), 16), B : 2 * B] = got
        return carry

    lax.fori_loop(0, NX, cols_of, 0)
    lags = jnp.dot(picked[...], picks[...], preferred_element_type=F32).astype(BF16)
    for n in range(NX):
        dense_cols[(2 * n + 1) * B : (2 * n + 2) * B, lanes] = lags[n * B : (n + 1) * B, :]

    def rows_of(n, carry):
        def put(j, got):
            dense_rows[pl.ds(pl.multiple_of(n * B + j, 16), 16), lanes] = got

        block(n // 4 * NZ + core * 4 + n % 4, put)
        return carry

    lax.fori_loop(0, 4 * NY, rows_of, 0)


def multiply(first, depth, dense_rows, dense_cols, inst, lag, row_sums, col_sums):
    def put(ref, index, value):
        if first:
            ref[index] = value
        else:
            ref[index] += value

    half = ROWS // 2
    for q in range(2):
        height = half + 16 * q
        out = lax.dot_general(
            dense_rows[q * half : q * half + height, 0:depth], dense_cols[:, 0:depth], NT,
            preferred_element_type=F32,
        )
        for h in range(2):
            part = out[h * 4 * B : (h + 1) * 4 * B]
            for x in range(NX):
                put(inst, (x, 2 * q + h), part[:, 2 * x * B : (2 * x + 1) * B])
                put(lag, (2 * q + h, x), part[:, (2 * x + 1) * B : (2 * x + 2) * B])
            put(row_sums, (2 * q + h,), part[:, COLS:])
        if q == 1:
            for n in range(2 * NX):
                put(col_sums, (n,), out[half : half + 8, n * B : (n + 1) * B])


def encode(value):
    top = jnp.max(jnp.abs(value), axis=0, keepdims=True)
    power = jnp.ceil(jnp.log(jnp.maximum(top, 1e-30)) * (STEPS / 0.6931471805599453))
    whole = jnp.floor(value * (jnp.exp2(power * (-1 / STEPS)) * TOP) + 0.5)
    return whole.astype(I32).astype(I16), power


def widen(ref, rows):
    return ref[rows, :].astype(I32).astype(F32)


def kernel(
    values, blocks, pairs, inst_out, lag_out,
    plain, index, ring, pair, dense_rows, dense_cols, picked, picks,
    inst, lag, row_sums, col_sums, powers, scales, out1, in1, out2, in2, sums0, sums1, sums2, between,
    ring_send, ring_recv, pair_send, pair_recv, rs_send, rs_recv, sum_send, sum_recv,
):
    x, y, z, core = place()

    def device(dx=0, dy=0, dz=0, dc=0):
        return (
            lax.rem(y + dy + NY, NY) * 2 + lax.rem(core + dc, 2),
            lax.rem(x + dx + NX, NX) * NZ + lax.rem(z + dz + NZ, NZ),
        )

    def send(source, target, send_sem, recv_sem, to):
        copy = pltpu.make_async_remote_copy(
            src_ref=source, dst_ref=target, send_sem=send_sem, recv_sem=recv_sem,
            device_id=to, device_id_type=MESH,
        )
        copy.start()
        return copy

    up, down, other = device(dz=1), device(dz=-1), device(dc=1)
    barrier = pltpu.get_barrier_semaphore()
    partners = [up, down, other]
    partners += [device(dx=d) for d in range(1, NX)] + [device(dy=d) for d in range(1, NY)]
    for to in partners:
        pl.semaphore_signal(barrier, inc=1, device_id=to, device_id_type=MESH)

    prepare(values, blocks, pairs, ring.at[0], plain, index)
    pl.semaphore_wait(barrier, len(partners))

    started = []

    def share(slot, rows, sem):
        started.append(
            send(ring.at[slot, rows], pair.at[slot, rows], pair_send.at[sem], pair_recv.at[sem], other)
        )
        return started[-1]

    whole = pl.ds(0, PACKET)
    low, high = pl.ds(0, HALF), pl.ds(HALF, PACKET - HALF)
    right = send(ring.at[0], ring.at[1], ring_send.at[1], ring_recv.at[1], up)
    left = send(ring.at[0], ring.at[4], ring_send.at[4], ring_recv.at[4], down)
    shared = share(0, whole, 0)

    dense_rows[ROWS:, :] = jnp.ones((16, 4 * B), BF16)
    dense_cols[COLS:, :] = jnp.ones((B, 4 * B), BF16)

    def fill_from(buffer, slot, position):
        lanes = pl.ds(position * B, B)
        fill(buffer.at[slot], lanes, core, z, dense_rows, dense_cols, picked, picks)

    def product(first, depth):
        multiply(first, depth, dense_rows, dense_cols, inst, lag, row_sums, col_sums)

    fill_from(ring, 0, 0)
    shared.wait_recv()
    fill_from(pair, 0, 1)
    product(True, 2 * B)

    for s in range(1, 4):
        right.wait_recv()
        started.append(right)
        if s < 3:
            right = send(ring.at[s], ring.at[s + 1], ring_send.at[s + 1], ring_recv.at[s + 1], up)
        else:
            right = send(ring.at[s, low], ring.at[7, low], ring_send.at[7], ring_recv.at[7], up)
        left.wait_recv()
        started.append(left)
        if s < 3:
            left = send(ring.at[3 + s], ring.at[4 + s], ring_send.at[4 + s], ring_recv.at[4 + s], down)
        else:
            left = send(ring.at[6, high], ring.at[7, high], ring_send.at[8], ring_recv.at[8], down)
        shared = [share(s, whole, s), share(3 + s, whole, 3 + s)]

        def from_ring(n, carry, s=s):
            fill_from(ring, s + 3 * n, n)
            return carry

        lax.fori_loop(0, 2, from_ring, 0)
        for copy in shared:
            copy.wait_recv()

        def from_pair(n, carry, s=s):
            fill_from(pair, s + 3 * n, 2 + n)
            return carry

        lax.fori_loop(0, 2, from_pair, 0)
        product(False, 4 * B)

    right.wait_recv()
    shared = [share(7, low, 7)]
    left.wait_recv()
    shared.append(share(7, high, 8))
    started += [right, left]
    fill_from(ring, 7, 0)
    for copy in shared:
        copy.wait_recv()
    fill_from(pair, 7, 1)
    product(False, 2 * B)

    accs = (inst, lag)
    at = ((x, y), (y, x))
    across = ((device(dx=1), device(dx=-1)), (device(dy=1), device(dy=-1)))
    ways = (across, (across[1], across[0]))

    def message(which, stage, kind, d):
        n = 2 * kind + d
        number = 6 * stage + n
        out, into = ((out1, in1), (out2, in2))[stage]
        copy = send(
            out.at[which, n], into.at[which, n],
            rs_send.at[which, number], rs_recv.at[which, number], ways[which][stage][d],
        )
        started.append(copy)
        return copy

    def scales_of(ref, data, slot):
        power = widen(ref, pl.ds(data, 16))
        scales[slot] = jnp.exp2(power * (1 / STEPS)) * (1 / TOP)

    def decoded(ref, n, slot):
        rows = pl.ds(pl.multiple_of(n * B, B), B)
        return widen(ref, rows) * scales[slot, pl.ds(n, 1), :]

    def write(ref, count, value_of):
        def body(n, carry):
            q, power = encode(value_of(n))
            ref[pl.ds(pl.multiple_of(n * B, B), B), :] = q
            powers[pl.ds(n, 1), :] = power
            return carry

        lax.fori_loop(0, count, body, 0)
        tail = jnp.concatenate([powers[...], jnp.zeros((8, B), F32)], axis=0)
        ref[count * B : count * B + 16, :] = tail.astype(I32).astype(I16)

    powers[...] = jnp.zeros_like(powers)
    col_means = [col_sums[n] * (1 / GROUP) for n in range(2 * NX)]
    for n in range(2 * NX):
        col_sums[n] = col_means[n]

    def centred(which, first, second, i):
        yy, xx = (second, first) if which == 0 else (first, second)
        rows = pl.ds(pl.multiple_of(i * B, B), B)
        mean = col_sums[2 * xx + which, 0:1, :]
        return accs[which][first, second, rows, :] - row_sums[yy, rows, :] * mean

    copies = {}
    for d in range(2):
        for which in range(2):
            first = lax.rem(at[which][0] + 2, 4)
            write(
                out1.at[which, d], 8,
                lambda n, which=which, first=first, d=d: centred(which, first, 2 * d + n // 4, n % 4),
            )
            copies[which, 0, d] = message(which, 0, 0, d)

    diagonal = lax.broadcasted_iota(I32, (B, B), 0) == lax.broadcasted_iota(I32, (B, B), 1)

    def sums_of(yy, carry):
        flat = []
        for i in range(4):
            tile = row_sums[yy, i * B : (i + 1) * B, :]
            flat.append(jnp.sum(jnp.where(diagonal, tile, 0.0), axis=0, keepdims=True))
        for xx in range(NX):
            means = [col_sums[2 * xx + w, 0:1, :] for w in range(2)]
            sums0[xx, yy] = jnp.concatenate(flat + means + means, axis=0)
        return carry

    lax.fori_loop(0, NY, sums_of, 0)
    exchange = []
    for d in range(1, NX):
        exchange.append(
            send(sums0.at[lax.rem(x + d, NX)], sums1.at[x], sum_send.at[d - 1], sum_recv.at[d - 1], device(dx=d))
        )
    sums1[x] = sums0[x]

    for d in range(2):
        for which in range(2):
            first = lax.rem(at[which][0] + 1 + 2 * d, 4)
            write(
                out1.at[which, 2 + d], 8,
                lambda n, which=which, first=first, d=d: centred(which, first, 2 - 2 * d + n // 4, n % 4),
            )
            copies[which, 1, d] = message(which, 0, 1, d)

    for copy in exchange:
        copy.wait_recv()
    started += exchange
    exchange = []
    for d in range(1, NY):
        exchange.append(
            send(
                sums1.at[:, lax.rem(y + d, NY)], sums2.at[pl.ds(pl.multiple_of(NX * y, NX), NX)],
                sum_send.at[2 + d], sum_recv.at[2 + d], device(dy=d),
            )
        )
    sums2[pl.ds(pl.multiple_of(NX * y, NX), NX)] = sums1[:, y]

    for d in range(2):
        for which in range(2):
            copies[which, 0, d].wait_recv()
            first = lax.rem(at[which][0] + 1 + 2 * d, 4)
            scales_of(in1.at[which, d], 8 * B, 0)
            write(
                out1.at[which, 4 + d], 8,
                lambda n, which=which, first=first, d=d: (
                    centred(which, first, 2 * d + n // 4, n % 4) + decoded(in1.at[which, d], n, 0)
                ),
            )
            copies[which, 2, d] = message(which, 0, 2, d)

    for copy in exchange:
        copy.wait_recv()
    started += exchange
    apart = []
    for n in range(6):
        of_groups = sums2[:, n, :]
        apart.append(of_groups - jnp.mean(of_groups, axis=0, keepdims=True))
    for which in range(2):
        for i in range(4):
            between[which, i * B : (i + 1) * B, :] = lax.dot_general(
                apart[i], apart[4 + which], TN,
                precision=lax.Precision.HIGHEST, preferred_element_type=F32,
            )

    for h in range(2):
        for which in range(2):
            a = at[which][0]
            parts = (4, 3) if h == 0 else (2, 5)
            for slot, n in enumerate(parts):
                copies[which, n // 2, n % 2].wait_recv()
                scales_of(in1.at[which, n], 8 * B, slot)

            def total(n, carry, which=which, a=a, h=h, parts=parts):
                second, i = 2 * h + n // 4, n % 4
                value = centred(which, a, second, i)
                for slot, part in enumerate(parts):
                    value = value + decoded(in1.at[which, part], n, slot)
                accs[which][a, second, pl.ds(pl.multiple_of(i * B, B), B), :] = value
                return carry

            lax.fori_loop(0, 8, total, 0)

    def summed(which, second, i):
        return accs[which][at[which][0], second, pl.ds(pl.multiple_of(i * B, B), B), :]

    for d in range(2):
        for which in range(2):
            second = lax.rem(at[which][1] + 2, 4)
            write(
                out2.at[which, d], 2,
                lambda n, which=which, second=second, d=d: summed(which, second, 2 * d + n),
            )
            copies[which, 0, d] = message(which, 1, 0, d)
    for d in range(2):
        for which in range(2):
            second = lax.rem(at[which][1] + 1 + 2 * d, 4)
            write(
                out2.at[which, 2 + d], 2,
                lambda n, which=which, second=second, d=d: summed(which, second, 2 - 2 * d + n),
            )
            copies[which, 1, d] = message(which, 1, 1, d)
    for d in range(2):
        for which in range(2):
            copies[which, 0, d].wait_recv()
            second = lax.rem(at[which][1] + 1 + 2 * d, 4)
            scales_of(in2.at[which, d], 2 * B, 0)
            write(
                out2.at[which, 4 + d], 2,
                lambda n, which=which, second=second, d=d: (
                    summed(which, second, 2 * d + n) + decoded(in2.at[which, d], n, 0)
                ),
            )
            copies[which, 2, d] = message(which, 1, 2, d)
    for h in range(2):
        for which in range(2):
            parts = (4, 3) if h == 0 else (2, 5)
            for slot, n in enumerate(parts):
                copies[which, n // 2, n % 2].wait_recv()
                scales_of(in2.at[which, n], 2 * B, slot)
            for n in range(2):
                rows = slice((2 * h + n) * B, (2 * h + n + 1) * B)
                value = summed(which, at[which][1], 2 * h + n) + between[which, rows, :]
                for slot, part in enumerate(parts):
                    value = value + decoded(in2.at[which, part], n, slot)
                (inst_out, lag_out)[which][rows, :] = value * (1 / PAIRS)
    for copy in started:
        copy.wait_send()


def on_device(frame_values, frame_blocks, lag_pairs):
    chunk = jax.ShapeDtypeStruct((4 * B, B), F32)
    vmem = pl.BlockSpec(memory_space=pltpu.VMEM)
    return pl.pallas_call(
        kernel,
        out_shape=(chunk, chunk),
        in_specs=[vmem] * 3,
        out_specs=(vmem, vmem),
        scratch_shapes=[
            pltpu.VMEM((FRAMES * SLOTS, B), F32),
            pltpu.VMEM((SLOTS, B), F32),
            pltpu.VMEM((NZ, PACKET, B), BF16),
            pltpu.VMEM((NZ, PACKET, B), BF16),
            pltpu.VMEM((ROWS + 16, 4 * B), BF16),
            pltpu.VMEM((COLS + B, 4 * B), BF16),
            pltpu.VMEM((NX * B, 2 * B), BF16),
            pltpu.VMEM((2 * B, B), BF16),
            pltpu.VMEM((NX, NY, 4 * B, B), F32),
            pltpu.VMEM((NY, NX, 4 * B, B), F32),
            pltpu.VMEM((NY, 4 * B, B), F32),
            pltpu.VMEM((2 * NX, 8, B), F32),
            pltpu.VMEM((8, B), F32),
            pltpu.VMEM((2, 16, B), F32),
            pltpu.VMEM((2, 6, FAR, B), I16),
            pltpu.VMEM((2, 6, FAR, B), I16),
            pltpu.VMEM((2, 6, NEAR, B), I16),
            pltpu.VMEM((2, 6, NEAR, B), I16),
            pltpu.VMEM((NX, NY, 8, B), F32),
            pltpu.VMEM((NX, NY, 8, B), F32),
            pltpu.VMEM((NX * NY, 8, B), F32),
            pltpu.VMEM((2, 4 * B, B), F32),
            pltpu.SemaphoreType.DMA((9,)),
            pltpu.SemaphoreType.DMA((9,)),
            pltpu.SemaphoreType.DMA((9,)),
            pltpu.SemaphoreType.DMA((9,)),
            pltpu.SemaphoreType.DMA((2, 12)),
            pltpu.SemaphoreType.DMA((2, 12)),
            pltpu.SemaphoreType.DMA((6,)),
            pltpu.SemaphoreType.DMA((6,)),
        ],
        compiler_params=pltpu.CompilerParams(
            collective_id=0, has_side_effects=True, vmem_limit_bytes=56 << 20
        ),
        name="covariances",
    )(frame_values, frame_blocks.T, lag_pairs.T)


def solution(mesh):
    spec = P(("traj", "feat"))
    return jax.shard_map(
        on_device,
        mesh=mesh,
        in_specs=(spec, spec, spec),
        out_specs=(P("traj", "feat"), P("traj", "feat")),
        check_vma=False,
    )
```

time: 124 us -> 79.9 us (0.64)
  Pallas kernels: 118 us -> 76.1 us
  other arithmetic: 3.32 us -> 0 us
    pallas_call x1, Pallas kernels: 118 us -> 76.1 us  [on_device(): pl.pallas_call(kernel, out_shape=(chunk, chunk), in_specs=[vmem] * 3, out...]
    sub x1 -> x0, other arithmetic: 1.95 us -> none  [on_device(): cov_lag = lag[:4 * B] / PAIRS - rows * (lag[4 * B + 4:4 * B + 5] / PAIRS)]
where the time goes in v2:
time: 79.9 us; the launch traced here: 79.2 us
  Pallas kernels  76.1 us (95%)
  local copies, waits for them, and re-layouts  2.42 us (3%)
    pallas_call x1, Pallas kernels, on_device(): pl.pallas_call(kernel, out_shape=(chunk, chunk), in_specs=[vmem] * 3, out...  76.1 us
    unnamed x4, local copies, waits for them, and re-layouts  2.42 us

profile of v2, /device:TPU:1, one launch (start us, length us, event | category | flops | bytes accessed | tf_op | source)
XLA Modules:
  0.0 79.2 jit_solution(8131363750405307972)
XLA Ops:
  0.6 76.1 %covariances.1 = (f32[512,128]{1,0:T(8,128)}, f32[512,128]{1,0:T(8,128)}) custom-call(bf16[160,8,128]{2,1,0:T(8,128)(2,1)} %values.1, s32[8,160]{1,0:T(8,128)} %bitcast.2, s32[2,128]{1,0:T(2,128)} %bitcast.3), custom_call_target="tpu_custom_call" | custom-call | tf_op jit(solution)/shard_map/covariances/pallas_call | solution.py:447
  76.7 0.0 copy-start
  76.8 1.7 %copy.7 = f32[512,128]{1,0:T(8,128)} copy(f32[512,128]{1,0:T(8,128)} %get-tuple-element.4) | data formatting | bytes 524288
  78.5 0.0 copy-done
  78.5 0.7 copy.8
Async XLA Ops:
  76.7 1.7 %copy-start = (f32[512,128]{1,0:T(8,128)S(1)}, f32[512,128]{1,0:T(8,128)}, u32[]{:S(2)}) copy-start(f32[512,128]{1,0:T(8,128)} %get-tuple-element.5) | copy-start | bytes 786436

commit v3 on v2

--- a/solution.py
+++ b/solution.py
@@ -19,7 +19,7 @@
 COLS = 2 * NX * B
 GROUP = 2 * NZ * B
 PAIRS = NX * NY * GROUP
-FAR = 8 * B + 16
+FAR = 4 * B + 16
 NEAR = 2 * B + 16
 STEPS = 16.0
 TOP = 32512.0
@@ -98,7 +98,7 @@
             picked[pl.ds(pl.multiple_of(n * B + j, 16), 16), B : 2 * B] = got
         return carry
 
-    lax.fori_loop(0, NX, cols_of, 0)
+    lax.fori_loop(0, NX, cols_of, 0, unroll=True)
     lags = jnp.dot(picked[...], picks[...], preferred_element_type=F32).astype(BF16)
     for n in range(NX):
         dense_cols[(2 * n + 1) * B : (2 * n + 2) * B, lanes] = lags[n * B : (n + 1) * B, :]
@@ -110,10 +110,10 @@
         block(n // 4 * NZ + core * 4 + n % 4, put)
         return carry
 
-    lax.fori_loop(0, 4 * NY, rows_of, 0)
-
-
-def multiply(first, depth, dense_rows, dense_cols, inst, lag, row_sums, col_sums):
+    lax.fori_loop(0, 4 * NY, rows_of, 0, unroll=True)
+
+
+def multiply(q, first, depth, dense_rows, dense_cols, inst, lag, row_sums, col_sums):
     def put(ref, index, value):
         if first:
             ref[index] = value
@@ -121,21 +121,20 @@
             ref[index] += value
 
     half = ROWS // 2
-    for q in range(2):
-        height = half + 16 * q
-        out = lax.dot_general(
-            dense_rows[q * half : q * half + height, 0:depth], dense_cols[:, 0:depth], NT,
-            preferred_element_type=F32,
-        )
-        for h in range(2):
-            part = out[h * 4 * B : (h + 1) * 4 * B]
-            for x in range(NX):
-                put(inst, (x, 2 * q + h), part[:, 2 * x * B : (2 * x + 1) * B])
-                put(lag, (2 * q + h, x), part[:, (2 * x + 1) * B : (2 * x + 2) * B])
-            put(row_sums, (2 * q + h,), part[:, COLS:])
-        if q == 1:
-            for n in range(2 * NX):
-                put(col_sums, (n,), out[half : half + 8, n * B : (n + 1) * B])
+    height = half + 16 * q
+    out = lax.dot_general(
+        dense_rows[q * half : q * half + height, 0:depth], dense_cols[:, 0:depth], NT,
+        preferred_element_type=F32,
+    )
+    for h in range(2):
+        part = out[h * 4 * B : (h + 1) * 4 * B]
+        for x in range(NX):
+            put(inst, (x, 2 * q + h), part[:, 2 * x * B : (2 * x + 1) * B])
+            put(lag, (2 * q + h, x), part[:, (2 * x + 1) * B : (2 * x + 2) * B])
+        put(row_sums, (2 * q + h,), part[:, COLS:])
+    if q == 1:
+        for n in range(2 * NX):
+            put(col_sums, (n,), out[half : half + 8, n * B : (n + 1) * B])
 
 
 def encode(value):
@@ -182,6 +181,25 @@
     pl.semaphore_wait(barrier, len(partners))
 
     started = []
+    low, high = pl.ds(0, HALF), pl.ds(HALF, PACKET - HALF)
+    pieces = ((low, high), (high, low))
+    ways = (up, down)
+    coming = {}
+
+    def pass_on(way, s, n):
+        rows = pieces[way][n]
+        held, there = (3 * way + s if s else 0), (3 * way + s + 1 if s < 3 else 7)
+        sem = 2 * there + (way if s == 3 else n)
+        coming[way, s + 1, n] = send(
+            ring.at[held, rows], ring.at[there, rows], ring_send.at[sem], ring_recv.at[sem], ways[way]
+        )
+        started.append(coming[way, s + 1, n])
+
+    def arrive(s, n):
+        for way in range(2):
+            coming[way, s, n].wait_recv()
+            if s < 3 or (s == 3 and n == 0):
+                pass_on(way, s, n)
 
     def share(slot, rows, sem):
         started.append(
@@ -190,9 +208,9 @@
         return started[-1]
 
     whole = pl.ds(0, PACKET)
-    low, high = pl.ds(0, HALF), pl.ds(HALF, PACKET - HALF)
-    right = send(ring.at[0], ring.at[1], ring_send.at[1], ring_recv.at[1], up)
-    left = send(ring.at[0], ring.at[4], ring_send.at[4], ring_recv.at[4], down)
+    for n in range(2):
+        for way in range(2):
+            pass_on(way, 0, n)
     shared = share(0, whole, 0)
 
     dense_rows[ROWS:, :] = jnp.ones((16, 4 * B), BF16)
@@ -202,27 +220,18 @@
         lanes = pl.ds(position * B, B)
         fill(buffer.at[slot], lanes, core, z, dense_rows, dense_cols, picked, picks)
 
-    def product(first, depth):
-        multiply(first, depth, dense_rows, dense_cols, inst, lag, row_sums, col_sums)
+    def product(q, first, depth):
+        multiply(q, first, depth, dense_rows, dense_cols, inst, lag, row_sums, col_sums)
 
     fill_from(ring, 0, 0)
     shared.wait_recv()
     fill_from(pair, 0, 1)
-    product(True, 2 * B)
+    product(0, True, 2 * B)
+    product(1, True, 2 * B)
+    arrive(1, 0)
 
     for s in range(1, 4):
-        right.wait_recv()
-        started.append(right)
-        if s < 3:
-            right = send(ring.at[s], ring.at[s + 1], ring_send.at[s + 1], ring_recv.at[s + 1], up)
-        else:
-            right = send(ring.at[s, low], ring.at[7, low], ring_send.at[7], ring_recv.at[7], up)
-        left.wait_recv()
-        started.append(left)
-        if s < 3:
-            left = send(ring.at[3 + s], ring.at[4 + s], ring_send.at[4 + s], ring_recv.at[4 + s], down)
-        else:
-            left = send(ring.at[6, high], ring.at[7, high], ring_send.at[8], ring_recv.at[8], down)
+        arrive(s, 1)
         shared = [share(s, whole, s), share(3 + s, whole, 3 + s)]
 
         def from_ring(n, carry, s=s):
@@ -238,42 +247,49 @@
             return carry
 
         lax.fori_loop(0, 2, from_pair, 0)
-        product(False, 4 * B)
-
-    right.wait_recv()
-    shared = [share(7, low, 7)]
-    left.wait_recv()
-    shared.append(share(7, high, 8))
-    started += [right, left]
+        product(0, False, 4 * B)
+        arrive(s + 1, 0)
+        if s == 3:
+            shared = [share(7, low, 7), share(7, high, 8)]
+        product(1, False, 4 * B)
+
     fill_from(ring, 7, 0)
     for copy in shared:
         copy.wait_recv()
     fill_from(pair, 7, 1)
-    product(False, 2 * B)
+    product(0, False, 2 * B)
+    product(1, False, 2 * B)
 
     accs = (inst, lag)
     at = ((x, y), (y, x))
     across = ((device(dx=1), device(dx=-1)), (device(dy=1), device(dy=-1)))
-    ways = (across, (across[1], across[0]))
-
-    def message(which, stage, kind, d):
-        n = 2 * kind + d
-        number = 6 * stage + n
+    routes = (across, (across[1], across[0]))
+    turns = ((2, 1), (3, 0))
+
+    def second_of(which, step):
+        return lax.rem(at[which][1] + step, 4)
+
+    def message(which, stage, n):
+        number = 12 * stage + n
+        d = (n // 2 if stage == 0 else n) % 2
         out, into = ((out1, in1), (out2, in2))[stage]
         copy = send(
             out.at[which, n], into.at[which, n],
-            rs_send.at[which, number], rs_recv.at[which, number], ways[which][stage][d],
+            rs_send.at[which, number], rs_recv.at[which, number], routes[which][stage][d],
         )
         started.append(copy)
-        return copy
-
-    def scales_of(ref, data, slot):
-        power = widen(ref, pl.ds(data, 16))
-        scales[slot] = jnp.exp2(power * (1 / STEPS)) * (1 / TOP)
-
-    def decoded(ref, n, slot):
-        rows = pl.ds(pl.multiple_of(n * B, B), B)
-        return widen(ref, rows) * scales[slot, pl.ds(n, 1), :]
+        copies[which, stage, n] = copy
+
+    def receive(which, stage, n):
+        copies[which, stage, n].wait_recv()
+        into, data = ((in1, 4 * B), (in2, 2 * B))[stage]
+        power = widen(into.at[which, n], pl.ds(data, 16))
+        scales[which, 12 * stage + n] = jnp.exp2(power * (1 / STEPS)) * (1 / TOP)
+
+    def decoded(which, stage, n, i):
+        into = (in1, in2)[stage]
+        rows = pl.ds(pl.multiple_of(i * B, B), B)
+        return widen(into.at[which, n], rows) * scales[which, 12 * stage + n, pl.ds(i, 1), :]
 
     def write(ref, count, value_of):
         def body(n, carry):
@@ -282,7 +298,7 @@
             powers[pl.ds(n, 1), :] = power
             return carry
 
-        lax.fori_loop(0, count, body, 0)
+        lax.fori_loop(0, count, body, 0, unroll=2)
         tail = jnp.concatenate([powers[...], jnp.zeros((8, B), F32)], axis=0)
         ref[count * B : count * B + 16, :] = tail.astype(I32).astype(I16)
 
@@ -298,14 +314,15 @@
         return accs[which][first, second, rows, :] - row_sums[yy, rows, :] * mean
 
     copies = {}
-    for d in range(2):
-        for which in range(2):
-            first = lax.rem(at[which][0] + 2, 4)
-            write(
-                out1.at[which, d], 8,
-                lambda n, which=which, first=first, d=d: centred(which, first, 2 * d + n // 4, n % 4),
-            )
-            copies[which, 0, d] = message(which, 0, 0, d)
+    for m in range(2):
+        for d in range(2):
+            for which in range(2):
+                first, second = lax.rem(at[which][0] + 2, 4), second_of(which, turns[d][m])
+                write(
+                    out1.at[which, 2 * d + m], 4,
+                    lambda i, w=which, f=first, s=second: centred(w, f, s, i),
+                )
+                message(which, 0, 2 * d + m)
 
     diagonal = lax.broadcasted_iota(I32, (B, B), 0) == lax.broadcasted_iota(I32, (B, B), 1)
 
@@ -327,14 +344,15 @@
         )
     sums1[x] = sums0[x]
 
-    for d in range(2):
-        for which in range(2):
-            first = lax.rem(at[which][0] + 1 + 2 * d, 4)
-            write(
-                out1.at[which, 2 + d], 8,
-                lambda n, which=which, first=first, d=d: centred(which, first, 2 - 2 * d + n // 4, n % 4),
-            )
-            copies[which, 1, d] = message(which, 0, 1, d)
+    for m in range(2):
+        for d in range(2):
+            for which in range(2):
+                first, second = lax.rem(at[which][0] + 1 + 2 * d, 4), second_of(which, turns[1 - d][m])
+                write(
+                    out1.at[which, 4 + 2 * d + m], 4,
+                    lambda i, w=which, f=first, s=second: centred(w, f, s, i),
+                )
+                message(which, 0, 4 + 2 * d + m)
 
     for copy in exchange:
         copy.wait_recv()
@@ -349,18 +367,19 @@
         )
     sums2[pl.ds(pl.multiple_of(NX * y, NX), NX)] = sums1[:, y]
 
-    for d in range(2):
-        for which in range(2):
-            copies[which, 0, d].wait_recv()
-            first = lax.rem(at[which][0] + 1 + 2 * d, 4)
-            scales_of(in1.at[which, d], 8 * B, 0)
-            write(
-                out1.at[which, 4 + d], 8,
-                lambda n, which=which, first=first, d=d: (
-                    centred(which, first, 2 * d + n // 4, n % 4) + decoded(in1.at[which, d], n, 0)
-                ),
-            )
-            copies[which, 2, d] = message(which, 0, 2, d)
+    for m in range(2):
+        for d in range(2):
+            for which in range(2):
+                n = 2 * d + m
+                receive(which, 0, n)
+                first, second = lax.rem(at[which][0] + 1 + 2 * d, 4), second_of(which, turns[d][m])
+                write(
+                    out1.at[which, 8 + n], 4,
+                    lambda i, w=which, f=first, s=second, n=n: (
+                        centred(w, f, s, i) + decoded(w, 0, n, i)
+                    ),
+                )
+                message(which, 0, 8 + n)
 
     for copy in exchange:
         copy.wait_recv()
@@ -376,67 +395,50 @@
                 precision=lax.Precision.HIGHEST, preferred_element_type=F32,
             )
 
-    for h in range(2):
-        for which in range(2):
-            a = at[which][0]
-            parts = (4, 3) if h == 0 else (2, 5)
-            for slot, n in enumerate(parts):
-                copies[which, n // 2, n % 2].wait_recv()
-                scales_of(in1.at[which, n], 8 * B, slot)
-
-            def total(n, carry, which=which, a=a, h=h, parts=parts):
-                second, i = 2 * h + n // 4, n % 4
-                value = centred(which, a, second, i)
-                for slot, part in enumerate(parts):
-                    value = value + decoded(in1.at[which, part], n, slot)
-                accs[which][a, second, pl.ds(pl.multiple_of(i * B, B), B), :] = value
-                return carry
-
-            lax.fori_loop(0, 8, total, 0)
-
-    def summed(which, second, i):
-        return accs[which][at[which][0], second, pl.ds(pl.multiple_of(i * B, B), B), :]
-
+    def gathered(which, d, m):
+        joint, near = 8 + 2 * d + m, 4 + 2 * (1 - d) + m
+        receive(which, 0, joint)
+        receive(which, 0, near)
+        second = second_of(which, turns[d][m])
+        return lambda i: (
+            centred(which, at[which][0], second, i) + decoded(which, 0, joint, i) + decoded(which, 0, near, i)
+        )
+
+    chunk = {}
+    for which in range(2):
+        chunk[which, 2] = gathered(which, 0, 0)
+        for d in range(2):
+            write(out2.at[which, d], 2, lambda n, w=which, d=d: chunk[w, 2](2 * d + n))
+            message(which, 1, d)
+    for which in range(2):
+        chunk[which, 3] = gathered(which, 1, 0)
+        write(out2.at[which, 3], 2, lambda n, w=which: chunk[w, 3](n))
+        message(which, 1, 3)
+    for which in range(2):
+        chunk[which, 1] = gathered(which, 0, 1)
+        write(out2.at[which, 2], 2, lambda n, w=which: chunk[w, 1](2 + n))
+        message(which, 1, 2)
     for d in range(2):
         for which in range(2):
-            second = lax.rem(at[which][1] + 2, 4)
-            write(
-                out2.at[which, d], 2,
-                lambda n, which=which, second=second, d=d: summed(which, second, 2 * d + n),
-            )
-            copies[which, 0, d] = message(which, 1, 0, d)
-    for d in range(2):
-        for which in range(2):
-            second = lax.rem(at[which][1] + 1 + 2 * d, 4)
-            write(
-                out2.at[which, 2 + d], 2,
-                lambda n, which=which, second=second, d=d: summed(which, second, 2 - 2 * d + n),
-            )
-            copies[which, 1, d] = message(which, 1, 1, d)
-    for d in range(2):
-        for which in range(2):
-            copies[which, 0, d].wait_recv()
-            second = lax.rem(at[which][1] + 1 + 2 * d, 4)
-            scales_of(in2.at[which, d], 2 * B, 0)
+            receive(which, 1, d)
             write(
                 out2.at[which, 4 + d], 2,
-                lambda n, which=which, second=second, d=d: (
-                    summed(which, second, 2 * d + n) + decoded(in2.at[which, d], n, 0)
-                ),
+                lambda n, w=which, d=d: chunk[w, 1 + 2 * d](2 * d + n) + decoded(w, 1, d, n),
             )
-            copies[which, 2, d] = message(which, 1, 2, d)
+            message(which, 1, 4 + d)
+    for which in range(2):
+        chunk[which, 0] = gathered(which, 1, 1)
     for h in range(2):
         for which in range(2):
             parts = (4, 3) if h == 0 else (2, 5)
-            for slot, n in enumerate(parts):
-                copies[which, n // 2, n % 2].wait_recv()
-                scales_of(in2.at[which, n], 2 * B, slot)
+            for part in parts:
+                receive(which, 1, part)
             for n in range(2):
-                rows = slice((2 * h + n) * B, (2 * h + n + 1) * B)
-                value = summed(which, at[which][1], 2 * h + n) + between[which, rows, :]
-                for slot, part in enumerate(parts):
-                    value = value + decoded(in2.at[which, part], n, slot)
-                (inst_out, lag_out)[which][rows, :] = value * (1 / PAIRS)
+                i = 2 * h + n
+                value = chunk[which, 0](i) + between[which, i * B : (i + 1) * B, :]
+                for part in parts:
+                    value = value + decoded(which, 1, part, n)
+                (inst_out, lag_out)[which][i * B : (i + 1) * B, :] = value * (1 / PAIRS)
     for copy in started:
         copy.wait_send()
 
@@ -463,21 +465,21 @@
             pltpu.VMEM((NY, 4 * B, B), F32),
             pltpu.VMEM((2 * NX, 8, B), F32),
             pltpu.VMEM((8, B), F32),
-            pltpu.VMEM((2, 16, B), F32),
-            pltpu.VMEM((2, 6, FAR, B), I16),
-            pltpu.VMEM((2, 6, FAR, B), I16),
+            pltpu.VMEM((2, 18, 16, B), F32),
+            pltpu.VMEM((2, 12, FAR, B), I16),
+            pltpu.VMEM((2, 12, FAR, B), I16),
             pltpu.VMEM((2, 6, NEAR, B), I16),
             pltpu.VMEM((2, 6, NEAR, B), I16),
             pltpu.VMEM((NX, NY, 8, B), F32),
             pltpu.VMEM((NX, NY, 8, B), F32),
             pltpu.VMEM((NX * NY, 8, B), F32),
             pltpu.VMEM((2, 4 * B, B), F32),
+            pltpu.SemaphoreType.DMA((2 * NZ,)),
+            pltpu.SemaphoreType.DMA((2 * NZ,)),
             pltpu.SemaphoreType.DMA((9,)),
             pltpu.SemaphoreType.DMA((9,)),
-            pltpu.SemaphoreType.DMA((9,)),
-            pltpu.SemaphoreType.DMA((9,)),
-            pltpu.SemaphoreType.DMA((2, 12)),
-            pltpu.SemaphoreType.DMA((2, 12)),
+            pltpu.SemaphoreType.DMA((2, 18)),
+            pltpu.SemaphoreType.DMA((2, 18)),
             pltpu.SemaphoreType.DMA((6,)),
             pltpu.SemaphoreType.DMA((6,)),
         ],

time: 79.9 us -> 74.3 us (0.930)
  Pallas kernels: 76.1 us -> 71.1 us
    pallas_call x1, Pallas kernels: 76.1 us -> 71.1 us  [on_device(): pl.pallas_call(kernel, out_shape=(chunk, chunk), in_specs=[vmem] * 3, out...]
where the time goes in v3:
time: 74.3 us; the launch traced here: 74.2 us
  Pallas kernels  71.1 us (96%)
  local copies, waits for them, and re-layouts  2.42 us (3%)
    pallas_call x1, Pallas kernels, on_device(): pl.pallas_call(kernel, out_shape=(chunk, chunk), in_specs=[vmem] * 3, out...  71.1 us
    unnamed x4, local copies, waits for them, and re-layouts  2.42 us

profile of v3, /device:TPU:1, one launch (start us, length us, event | category | flops | bytes accessed | tf_op | source)
XLA Modules:
  0.0 74.2 jit_solution(9892787144071585538)
XLA Ops:
  0.6 71.1 %covariances.1 = (f32[512,128]{1,0:T(8,128)}, f32[512,128]{1,0:T(8,128)}) custom-call(bf16[160,8,128]{2,1,0:T(8,128)(2,1)} %values.1, s32[8,160]{1,0:T(8,128)} %bitcast.2, s32[2,128]{1,0:T(2,128)} %bitcast.3), custom_call_target="tpu_custom_call" | custom-call | tf_op jit(solution)/shard_map/covariances/pallas_call | solution.py:449
  71.8 0.0 copy-start
  71.8 1.7 %copy.7 = f32[512,128]{1,0:T(8,128)} copy(f32[512,128]{1,0:T(8,128)} %get-tuple-element.4) | data formatting | bytes 524288
  73.5 0.0 copy-done
  73.5 0.7 copy.8
Async XLA Ops:
  71.8 1.7 %copy-start = (f32[512,128]{1,0:T(8,128)S(1)}, f32[512,128]{1,0:T(8,128)}, u32[]{:S(2)}) copy-start(f32[512,128]{1,0:T(8,128)} %get-tuple-element.5) | copy-start | bytes 786436

commit v4 on v3

--- a/solution.py
+++ b/solution.py
@@ -149,7 +149,7 @@
 
 
 def kernel(
-    values, blocks, pairs, inst_out, lag_out,
+    values_in, blocks_in, pairs_in, inst_out, lag_out, values, blocks, pairs, load,
     plain, index, ring, pair, dense_rows, dense_cols, picked, picks,
     inst, lag, row_sums, col_sums, powers, scales, out1, in1, out2, in2, sums0, sums1, sums2, between,
     ring_send, ring_recv, pair_send, pair_recv, rs_send, rs_recv, sum_send, sum_recv,
@@ -171,12 +171,18 @@
         return copy
 
     up, down, other = device(dz=1), device(dz=-1), device(dc=1)
+    loads = []
+    for n, (source, target) in enumerate(((values_in, values), (blocks_in, blocks), (pairs_in, pairs))):
+        loads.append(pltpu.make_async_copy(source, target, load.at[n]))
+        loads[-1].start()
     barrier = pltpu.get_barrier_semaphore()
     partners = [up, down, other]
     partners += [device(dx=d) for d in range(1, NX)] + [device(dy=d) for d in range(1, NY)]
     for to in partners:
         pl.semaphore_signal(barrier, inc=1, device_id=to, device_id_type=MESH)
 
+    for copy in loads:
+        copy.wait()
     prepare(values, blocks, pairs, ring.at[0], plain, index)
     pl.semaphore_wait(barrier, len(partners))
 
@@ -449,9 +455,13 @@
     return pl.pallas_call(
         kernel,
         out_shape=(chunk, chunk),
-        in_specs=[vmem] * 3,
+        in_specs=[pl.BlockSpec(memory_space=pltpu.HBM)] * 3,
         out_specs=(vmem, vmem),
         scratch_shapes=[
+            pltpu.VMEM((FRAMES, SLOTS, B), BF16),
+            pltpu.VMEM((SLOTS, FRAMES), I32),
+            pltpu.VMEM((2, B), I32),
+            pltpu.SemaphoreType.DMA((3,)),
             pltpu.VMEM((FRAMES * SLOTS, B), F32),
             pltpu.VMEM((SLOTS, B), F32),
             pltpu.VMEM((NZ, PACKET, B), BF16),

time: 74.3 us -> 73.4 us (0.988)
  Pallas kernels: 71.1 us -> 70.2 us
    pallas_call x1, Pallas kernels: 71.1 us -> 70.2 us  [on_device(): pl.pallas_call(kernel, out_shape=(chunk, chunk), in_specs=[pl.BlockSpec(m...]
where the time goes in v4:
time: 73.4 us; the launch traced here: 73.3 us
  Pallas kernels  70.2 us (96%)
  local copies, waits for them, and re-layouts  2.42 us (3%)
    pallas_call x1, Pallas kernels, on_device(): pl.pallas_call(kernel, out_shape=(chunk, chunk), in_specs=[pl.BlockSpec(m...  70.2 us
    unnamed x4, local copies, waits for them, and re-layouts  2.42 us

profile of v4, /device:TPU:1, one launch (start us, length us, event | category | flops | bytes accessed | tf_op | source)
XLA Modules:
  0.0 73.3 jit_solution(17736979578218382255)
XLA Ops:
  0.6 70.2 %covariances.1 = (f32[512,128]{1,0:T(8,128)}, f32[512,128]{1,0:T(8,128)}) custom-call(bf16[160,8,128]{2,1,0:T(8,128)(2,1)} %values_in.1, s32[8,160]{1,0:T(8,128)} %bitcast.2, s32[2,128]{1,0:T(2,128)} %bitcast.3), custom_call_target="tpu_custom_call" | custom-call | tf_op jit(solution)/shard_map/covariances/pallas_call | solution.py:455
  70.8 0.0 copy-start
  70.9 1.7 %copy.7 = f32[512,128]{1,0:T(8,128)} copy(f32[512,128]{1,0:T(8,128)} %get-tuple-element.4) | data formatting | bytes 524288
  72.6 0.0 copy-done
  72.6 0.7 copy.8
Async XLA Ops:
  70.8 1.7 %copy-start = (f32[512,128]{1,0:T(8,128)S(1)}, f32[512,128]{1,0:T(8,128)}, u32[]{:S(2)}) copy-start(f32[512,128]{1,0:T(8,128)} %get-tuple-element.5) | copy-start | bytes 786436

commit v5 on v4

--- a/solution.py
+++ b/solution.py
@@ -304,7 +304,7 @@
             powers[pl.ds(n, 1), :] = power
             return carry
 
-        lax.fori_loop(0, count, body, 0, unroll=2)
+        lax.fori_loop(0, count, body, 0, unroll=True)
         tail = jnp.concatenate([powers[...], jnp.zeros((8, B), F32)], axis=0)
         ref[count * B : count * B + 16, :] = tail.astype(I32).astype(I16)
 

time: 73.4 us -> 73.2 us (level)
  no operation moved by 1% of the time
where the time goes in v5:
time: 73.2 us; the launch traced here: 73.1 us
  Pallas kernels  70 us (96%)
  local copies, waits for them, and re-layouts  2.42 us (3%)
    pallas_call x1, Pallas kernels, on_device(): pl.pallas_call(kernel, out_shape=(chunk, chunk), in_specs=[pl.BlockSpec(m...  70 us
    unnamed x4, local copies, waits for them, and re-layouts  2.42 us

profile of v5, /device:TPU:1, one launch (start us, length us, event | category | flops | bytes accessed | tf_op | source)
XLA Modules:
  0.0 73.1 jit_solution(8366190532656455936)
XLA Ops:
  0.6 70.0 %covariances.1 = (f32[512,128]{1,0:T(8,128)}, f32[512,128]{1,0:T(8,128)}) custom-call(bf16[160,8,128]{2,1,0:T(8,128)(2,1)} %values_in.1, s32[8,160]{1,0:T(8,128)} %bitcast.2, s32[2,128]{1,0:T(2,128)} %bitcast.3), custom_call_target="tpu_custom_call" | custom-call | tf_op jit(solution)/shard_map/covariances/pallas_call | solution.py:455
  70.7 0.0 copy-start
  70.7 1.7 %copy.7 = f32[512,128]{1,0:T(8,128)} copy(f32[512,128]{1,0:T(8,128)} %get-tuple-element.4) | data formatting | bytes 524288
  72.4 0.0 copy-done
  72.4 0.7 copy.8
Async XLA Ops:
  70.7 1.7 %copy-start = (f32[512,128]{1,0:T(8,128)S(1)}, f32[512,128]{1,0:T(8,128)}, u32[]{:S(2)}) copy-start(f32[512,128]{1,0:T(8,128)} %get-tuple-element.5) | copy-start | bytes 786436
